TPU v7x, 32 devices: a whole 2x2x4 slice. The times are simulated.
32 devices in a mesh: seq: 16 (over z, y, core), head: 2 (over x).
Axes of the slice: x: 2, y: 2, z: 4, core: 2. Of those that a mesh axis runs over, the one named last changes fastest.
Arguments:
- queries: bfloat16 [6144, 768], P('seq', 'head'), as said below
- keys: bfloat16 [6144, 768], P('seq', 'head'), as said below
- values: bfloat16 [6144, 768], P('seq', 'head'), may hold values from -6 to 6
- image_tiles: int32 [5], replicated, may hold values from 1 to 21, 48 in all
Outputs:
- attended: bfloat16 [6144, 768], P(('seq', 'head'))
Inputs may be any that keep to these rules, and one draw needn't show every extreme that they name: `image_tiles`: the 5 images fill all 48 tiles in order; the longest holds exactly 21 tiles. `queries`: entries lie within -6 and 6. `keys`: entries lie within -6 and 6.
All inputs are finite; a program needn't handle non-finite values.
Results may differ from a plain program's by a relative error of at most 0.007.
Values may be sent and summed in bfloat16 or wider, within the bound.
No kernel may reach another device: no remote copies, remote signals or barrier semaphores. Data moves between devices by JAX's collectives and lax.ppermute only.
A program may use at most 64 MiB of HBM per device.

v0:
```python
import functools
import math

import jax
import jax.numpy as jnp
from jax import lax
from jax.experimental import pallas as pl
from jax.experimental.pallas import tpu as pltpu
from jax.sharding import PartitionSpec as P

HEAD_DIM = 128
TILE = 128
MOST_TILES = 21

LOWEST = -1e30
SCALE2 = math.log2(math.e) / math.sqrt(HEAD_DIM)

VMEM = pl.BlockSpec(memory_space=pltpu.VMEM)
SMEM = pl.BlockSpec(memory_space=pltpu.SMEM)


def params():
    return pltpu.CompilerParams(vmem_limit_bytes=32 * 1024 * 1024)


def pack_kernel(k_ref, v_ref, out_ref):
    rows, columns = k_ref.shape
    out_ref[:rows, :columns] = k_ref[...]
    out_ref[rows:, :rows] = v_ref[...].T


def pack(keys, values):
    rows, columns = keys.shape
    return pl.pallas_call(
        pack_kernel,
        out_shape=jax.ShapeDtypeStruct((rows + columns, max(rows, columns)), keys.dtype),
        in_specs=[VMEM, VMEM],
        out_specs=VMEM,
        compiler_params=params(),
        name="pack",
    )(keys, values)


def image_bounds(tiles_ref, tile):
    first = jnp.int32(0)
    start, end = jnp.int32(0), jnp.int32(0)
    for i in range(tiles_ref.shape[0]):
        after = first + tiles_ref[i]
        inside = (tile >= first) & (tile < after)
        start = jnp.where(inside, first, start)
        end = jnp.where(inside, after, end)
        first = after
    return start, end


def attend_kernel(halves, slots, fresh, rows, columns, tiles_ref, owners_ref, *refs):
    heads = columns // HEAD_DIM
    tiles = rows // TILE
    q_refs, refs = refs[:halves], refs[halves:]
    slot_refs, refs = refs[: len(slots)], refs[len(slots) :]
    if fresh:
        old_refs, new_refs = refs, refs
    else:
        old_refs, new_refs = refs[:halves], refs[halves:]

    for half in range(halves):
        q_ref, old_ref, new_ref = q_refs[half], old_refs[half], new_refs[half]
        if fresh:
            new_ref[:columns] = jnp.zeros((columns, rows), jnp.float32)
            new_ref[columns : columns + heads] = jnp.full((heads, rows), LOWEST, jnp.float32)
            new_ref[columns + heads :] = jnp.zeros((new_ref.shape[0] - columns - heads, rows), jnp.float32)
        else:
            new_ref[...] = old_ref[...]

        @pl.loop(0, tiles)
        def _(at):
            lanes = pl.ds(pl.multiple_of(at * TILE, TILE), TILE)
            start, end = image_bounds(tiles_ref, owners_ref[half] * tiles + at)
            for slot_ref, owner_at in zip(slot_refs, slots):
                first = owners_ref[owner_at] * tiles

                @pl.when((first < end) & (first + tiles > start))
                def _():
                    off = [
                        jnp.where((first + j >= start) & (first + j < end), 0.0, -LOWEST).astype(jnp.float32)
                        for j in range(tiles)
                    ]
                    for h in range(heads):
                        columns_h = slice(h * HEAD_DIM, (h + 1) * HEAD_DIM)
                        scores = lax.dot_general(
                            slot_ref[:rows, columns_h],
                            q_ref[lanes, columns_h],
                            (((1,), (1,)), ((), ())),
                            preferred_element_type=jnp.float32,
                        )
                        parts = [scores[j * TILE : (j + 1) * TILE] for j in range(tiles)]
                        old_max = new_ref[columns + h : columns + h + 1, lanes]
                        new_max = old_max
                        for j in range(tiles):
                            new_max = jnp.maximum(new_max, jnp.max(parts[j], axis=0, keepdims=True) - off[j])
                        scaled = new_max * SCALE2
                        weights = [jnp.exp2(parts[j] * SCALE2 - (scaled + off[j])) for j in range(tiles)]
                        factor = jnp.exp2((old_max - new_max) * SCALE2)
                        total = functools.reduce(jnp.add, weights)
                        total = jnp.sum(total, axis=0, keepdims=True)
                        rounded = jnp.concatenate([w.astype(jnp.bfloat16) for w in weights], axis=0)
                        update = jnp.dot(
                            slot_ref[rows + h * HEAD_DIM : rows + (h + 1) * HEAD_DIM, :rows],
                            rounded,
                            preferred_element_type=jnp.float32,
                        )
                        at_total = slice(columns + heads + h, columns + heads + h + 1)
                        new_ref[columns_h, lanes] = new_ref[columns_h, lanes] * factor + update
                        new_ref[columns + h : columns + h + 1, lanes] = new_max
                        new_ref[at_total, lanes] = new_ref[at_total, lanes] * factor + total


def attend(image_tiles, owners, queries, blocks, slots, states):
    halves = len(queries)
    rows, columns = queries[0].shape
    heads = columns // HEAD_DIM
    state_rows = columns + -(-2 * heads // 8) * 8
    shape = jax.ShapeDtypeStruct((state_rows, rows), jnp.float32)
    fresh = not states
    pairs = halves * (rows // TILE) ** 2 * heads * len(blocks)
    return pl.pallas_call(
        functools.partial(attend_kernel, halves, slots, fresh, rows, columns),
        out_shape=[shape] * halves,
        in_specs=[SMEM, SMEM] + [VMEM] * (halves + len(blocks) + len(states)),
        out_specs=[VMEM] * halves,
        compiler_params=params(),
        cost_estimate=pl.CostEstimate(
            flops=pairs * 4 * TILE * TILE * HEAD_DIM,
            bytes_accessed=len(blocks) * rows * columns * 4 + 4 * halves * state_rows * rows,
            transcendentals=pairs * TILE * TILE,
        ),
        name="attend",
    )(image_tiles, owners, *queries, *blocks, *states)


def finish_kernel(states, rows, columns, *refs):
    heads = columns // HEAD_DIM
    out_ref = refs[states]
    for h in range(heads):
        columns_h = slice(h * HEAD_DIM, (h + 1) * HEAD_DIM)
        maxima = [refs[i][columns + h : columns + h + 1] for i in range(states)]
        totals = [refs[i][columns + heads + h : columns + heads + h + 1] for i in range(states)]
        largest = functools.reduce(jnp.maximum, maxima)
        factors = [jnp.exp2((m - largest) * SCALE2) for m in maxima]
        total = functools.reduce(jnp.add, [f * t for f, t in zip(factors, totals)])
        summed = functools.reduce(jnp.add, [refs[i][columns_h] * (factors[i] / total) for i in range(states)])
        out_ref[:, columns_h] = summed.T.astype(out_ref.dtype)


def finish(states, rows, columns):
    return pl.pallas_call(
        functools.partial(finish_kernel, len(states), rows, columns),
        out_shape=jax.ShapeDtypeStruct((rows, columns), jnp.bfloat16),
        in_specs=[VMEM] * len(states),
        out_specs=VMEM,
        compiler_params=params(),
        name="finish",
    )(*states)


def chip_pairs(mesh):
    places = [tuple(getattr(d, "coords", ())) for d in mesh.devices[:, 0]]
    count = len(places)
    if count % 4 or not places[0]:
        return False
    cores = all(places[i] == places[i + 1] for i in range(0, count, 2))
    level = all(places[i][2] == places[i + 3][2] for i in range(0, count, 4))
    climb = all(places[i][2] != places[i + 4][2] for i in range(0, count - 4))
    return cores and level and climb


def paired_shards(owner_count, queries, keys, values, image_tiles):
    rows, columns = queries.shape
    tiles = rows // TILE
    every = range(owner_count)

    def sign(s):
        return 1 - 2 * ((s // 2) % 2)

    def moved(array, source):
        return lax.ppermute(array, "seq", [(source(s), s) for s in every if 0 <= source(s) < owner_count])

    along = lambda s: s + 4 * sign(s)
    against = lambda s: s - 4 * sign(s)
    across = lambda s: s + 2 * sign(s)
    corner = lambda s: s + 8 * (1 - 2 * (s % 2))
    sibling = lambda s: s + 1 - 2 * (s % 2)

    me = lax.axis_index("seq")
    owners = jnp.stack(
        [
            me,
            sibling(me),
            along(me),
            against(me),
            across(me),
            me - 2 * sign(me),
            me + 6 * sign(me),
            me - 6 * sign(me),
            corner(me),
        ]
    ).astype(jnp.int32)

    ends = jnp.cumsum(image_tiles)
    chip_tiles = 2 * tiles
    first_chip = (ends - image_tiles) // chip_tiles
    last_chip = (ends - 1) // chip_tiles
    odd_chip = first_chip + 1 - first_chip % 2
    far = jnp.where(last_chip - first_chip >= 4, 2, jnp.where(last_chip - odd_chip >= 3, 1, 0))
    far = jnp.max(far).astype(jnp.int32)

    block = pack(keys, values)
    a1 = moved(block, along)
    b1 = moved(block, against)
    y1 = moved(block, across)
    other = moved(queries, sibling)
    both = (queries, other)

    fold = functools.partial(attend, image_tiles, owners, both)
    states = fold([block], [0], [])
    ya = moved(a1, across)
    ay = moved(y1, along)
    states = fold([a1, b1, y1], [2, 3, 4], states)

    def near(block, ya, ay, states):
        return fold([ya, ay], [5, 6], states)

    def further(block, ya, ay, states):
        bya = moved(ya, against)
        states = fold([ya, ay], [5, 6], states)
        return fold([bya], [7], states)

    def furthest(block, ya, ay, states):
        bya = moved(ya, against)
        corner_block = moved(block, corner)
        states = fold([ya, ay], [5, 6], states)
        return fold([bya, corner_block], [7, 8], states)

    mine, theirs = lax.switch(far, [near, further, furthest], block, ya, ay, states)
    return finish([mine, moved(theirs, sibling)], rows, columns)


def ring_shards(owner_count, queries, keys, values, image_tiles):
    rows, columns = queries.shape
    reach = min(owner_count - 1, -(-(MOST_TILES - 1) // (rows // TILE)))
    me = lax.axis_index("seq")
    block = pack(keys, values)
    owners = jnp.stack([me] + [me - k for k in range(1, reach + 1)] + [me + k for k in range(1, reach + 1)])
    owners = owners.astype(jnp.int32)
    fold = functools.partial(attend, image_tiles, owners, (queries,))
    up = [(i, i + 1) for i in range(owner_count - 1)]
    down = [(i + 1, i) for i in range(owner_count - 1)]
    below = above = block
    states = []
    held, slots = [block], [0]
    for k in range(1, reach + 1):
        below = lax.ppermute(below, "seq", up)
        above = lax.ppermute(above, "seq", down)
        states = fold(held, slots, states)
        held, slots = [below, above], [k, reach + k]
    states = fold(held, slots, states)
    return finish(states, rows, columns)


def solution(mesh):
    owner_count = mesh.shape["seq"]
    plan = paired_shards if chip_pairs(mesh) else ring_shards

    def shards(queries, keys, values, image_tiles):
        attended = plan(owner_count, queries, keys, values, image_tiles)
        return lax.all_to_all(attended, "head", split_axis=0, concat_axis=1, tiled=True)

    placed = (P("seq", "head"), P("seq", "head"), P("seq", "head"), P())
    return jax.shard_map(
        shards, mesh=mesh, in_specs=placed, out_specs=P(("seq", "head"), None), check_vma=False
    )
```

profile of v0, /device:TPU:16, one launch (start us, length us, event | category | flops | bytes accessed | tf_op | source)
XLA Modules:
  0.0 51.5 jit_solution(233887237902686561)
XLA Ops:
  0.0 0.0 copy-start
  0.0 1.0 %copy-done = bf16[384,384]{1,0:T(8,128)(2,1)S(1)} copy-done((bf16[384,384]{1,0:T(8,128)(2,1)S(1)}, bf16[384,384]{1,0:T(8,128)(2,1)}, u32[]{:S(2)}) %copy-start) | copy-done | bytes 294936
  1.0 0.0 copy-start.1
  1.0 1.0 %copy-done.1 = bf16[384,384]{1,0:T(8,128)(2,1)S(1)} copy-done((bf16[384,384]{1,0:T(8,128)(2,1)S(1)}, bf16[384,384]{1,0:T(8,128)(2,1)}, u32[]{:S(2)}) %copy-start.1) | copy-done | bytes 294936
  1.9 0.0 copy-start.2
  1.9 0.1 pack.1.refs_2_
  2.1 1.6 %collective-permute-start.6 = (bf16[768,384]{1,0:T(8,128)(2,1)S(1)}, bf16[768,384]{1,0:T(8,128)(2,1)S(1)}, u32[]{:S(2)}, u32[]{:S(2)}) collective-permute-start(bf16[768,384]{1,0:T(8,128)(2,1)S(1)} %pack.1.refs_2_), channel_id=1, source_target_pairs={{4,0},{6,2},{0,4},{2,6},{12,8},{14,10},{8,12},{10,14},{20,16},{22,... | collective-permute-start | bytes 1769480 | tf_op jit(solution)/shard_map/ppermute | solution.py:186
  3.7 2.3 %collective-permute-start.4 = (bf16[768,384]{1,0:T(8,128)(2,1)S(1)}, bf16[768,384]{1,0:T(8,128)(2,1)S(1)}, u32[]{:S(2)}, u32[]{:S(2)}) collective-permute-start(bf16[768,384]{1,0:T(8,128)(2,1)S(1)} %pack.1.refs_2_), channel_id=1, source_target_pairs={{8,0},{10,2},{16,8},{18,10},{4,12},{6,14},{24,16},{26,18},{12,20},... | collective-permute-start | bytes 1769480 | tf_op jit(solution)/shard_map/ppermute | solution.py:186
  6.0 3.5 %collective-permute-start.8 = (bf16[768,384]{1,0:T(8,128)(2,1)S(1)}, bf16[768,384]{1,0:T(8,128)(2,1)S(1)}, u32[]{:S(2)}, u32[]{:S(2)}) collective-permute-start(bf16[768,384]{1,0:T(8,128)(2,1)S(1)} %pack.1.refs_2_), channel_id=1, source_target_pairs={{12,4},{14,6},{0,8},{2,10},{20,12},{22,14},{8,16},{10,18},{28,20},... | collective-permute-start | bytes 1769480 | tf_op jit(solution)/shard_map/ppermute | solution.py:186
  9.5 7.7 %collective-permute-done.6.refs_4_ = bf16[768,384]{1,0:T(8,128)(2,1)S(1)} collective-permute-done((bf16[768,384]{1,0:T(8,128)(2,1)S(1)}, bf16[768,384]{1,0:T(8,128)(2,1)S(1)}, u32[]{:S(2)}, u32[]{:S(2)}) %collective-permute-start.6) | collective-permute-done | bytes 589856 | tf_op jit(solution)/shard_map/ppermute | solution.py:186
  17.2 2.3 %collective-permute-start.7 = (bf16[768,384]{1,0:T(8,128)(2,1)S(1)}, bf16[768,384]{1,0:T(8,128)(2,1)S(1)}, u32[]{:S(2)}, u32[]{:S(2)}) collective-permute-start(bf16[768,384]{1,0:T(8,128)(2,1)S(1)} %collective-permute-done.6.refs_4_), channel_id=1, source_target_pairs={{8,0},{10,2},{16,8},{18,10},{4,12},{6,14},{24,16},{26,18},{12,20},... | collective-permute-start | bytes 1769480 | tf_op jit(solution)/shard_map/ppermute | solution.py:186
  19.6 0.8 %collective-permute-done.4.refs_2_ = bf16[768,384]{1,0:T(8,128)(2,1)S(1)} collective-permute-done((bf16[768,384]{1,0:T(8,128)(2,1)S(1)}, bf16[768,384]{1,0:T(8,128)(2,1)S(1)}, u32[]{:S(2)}, u32[]{:S(2)}) %collective-permute-start.4) | collective-permute-done | bytes 589856 | tf_op jit(solution)/shard_map/ppermute | solution.py:186
  20.3 2.0 %collective-permute-start.5 = (bf16[768,384]{1,0:T(8,128)(2,1)S(1)}, bf16[768,384]{1,0:T(8,128)(2,1)}, u32[]{:S(2)}, u32[]{:S(2)}) collective-permute-start(bf16[768,384]{1,0:T(8,128)(2,1)S(1)} %collective-permute-done.4.refs_2_), channel_id=1, source_target_pairs={{4,0},{6,2},{0,4},{2,6},{12,8},{14,10},{8,12},{10,14},{20,16},{22,... | collective-permute-start | bytes 1769480 | tf_op jit(solution)/shard_map/ppermute | solution.py:186
  22.3 0.0 copy-done.2
  22.3 0.0 collective-permute-start.3
  22.3 0.0 copy-start.3
  22.3 0.7 %copy-done.3 = s32[5]{0:T(128)S(1)} copy-done((s32[5]{0:T(128)S(1)}, s32[5]{0:T(128)}, u32[]{:S(2)}) %copy-start.3) | copy-done | bytes 44
  22.9 0.2 reduce-window.9
  23.1 0.7 %fusion.2 = s32[]{:T(128)} fusion(s32[5]{0:T(128)S(1)} %copy-done.3, s32[5,1]{0,1:T(1,128)S(1)} %reduce-window.9), kind=kLoop, calls=%fused_computation.9 | loop fusion | flops 189 | bytes 44 | tf_op jit(solution)/shard_map/reduce_max | solution.py:215
  24.4 0.1 stack.39.owners_ref
  24.5 0.0 collective-permute-done.3.refs_1_
  24.5 3.8 %attend.12 = (f32[392,384]{1,0:T(8,128)S(1)}, f32[392,384]{1,0:T(8,128)S(1)}) custom-call(s32[5]{0:T(128)S(1)} %copy-done.3, s32[9]{0:T(128)S(1)} %stack.39.owners_ref, bf16[384,384]{1,0:T(8,128)(2,1)S(1)} %copy-done.2, bf16[384,384]{1,0:T(8,128)(2,1)S(1)} %collective-permute-done.3.refs_1_, bf16[768,384]{1,0:T(8,128)(2,1)S(1)} %pack.1.refs_2_), custom_call_target="tpu_custom_call" | custom-call | flops 452984832 | bytes 1794048 | tf_op jit(solution)/shard_map/attend/pallas_call | solution.py:126
  28.3 0.0 collective-permute-done.8.refs_3_
  28.4 7.0 %attend.13 = (f32[392,384]{1,0:T(8,128)S(1)}, f32[392,384]{1,0:T(8,128)S(1)}) custom-call(s32[5]{0:T(128)S(1)} %copy-done.3, s32[9]{0:T(128)S(1)} %stack.39.owners_ref, bf16[384,384]{1,0:T(8,128)(2,1)S(1)} %copy-done.2, bf16[384,384]{1,0:T(8,128)(2,1)S(1)} %collective-permute-done.3.refs_1_, bf16[768,384]{1,0:T(8,128)(2,1)S(1)} %collective-permute-done.4.refs_2_, ...), custom_call_target="tpu_custom_call" | custom-call | flops 1358954496 | bytes 2973696 | tf_op jit(solution)/shard_map/attend/pallas_call | solution.py:126
  35.3 0.0 collective-permute-done.7
  35.4 0.0 collective-permute-done.5
  35.4 4.6 %conditional.1 = ((f32[392,384]{1,0:T(8,128)S(1)}, f32[392,384]{1,0:T(8,128)S(1)})) conditional(s32[]{:T(128)} %clamp.3, (s32[5]{0:T(128)S(1)}, s32[9]{0:T(128)S(1)}, bf16[384,384]{1,0:T(8,128)(2,1)S(1)}, bf16[384,384]{1,0:T(8,128)(2,1)S(1)}, bf16[768,384]{1,0:T(8,128)(2,1)}, /*index=5*/bf16[768,384]{1,0:T(8,128)(2,1)S(1)}, ...), branch_computations={%region_2.3_spmd, %region_3.4_spmd, %region_4.5_spmd} | conditional | flops 1811939328 | bytes 14303376 | solution.py:244
  35.4 4.4 %attend.7 = (f32[392,384]{1,0:T(8,128)S(1)}, f32[392,384]{1,0:T(8,128)S(1)}) custom-call(s32[5]{0:T(128)S(1)} %get-tuple-element.55.tiles_ref, s32[9]{0:T(128)S(1)} %get-tuple-element.56.owners_ref, bf16[384,384]{1,0:T(8,128)(2,1)S(1)} %get-tuple-element.57.refs_0_, bf16[384,384]{1,0:T(8,128)(2,1)S(1)} %get-tuple-element.58.refs_1_, ...), custom_call_target="tpu_custom_call" | custom-call | flops 905969664 | bytes 2383872 | tf_op jit(solution)/shard_map/cond/branch_0_fun/attend/pallas_call | solution.py:126
  40.0 0.1 collective-permute-start.9
  40.1 2.0 %collective-permute-done.9.refs_1_ = f32[392,384]{1,0:T(8,128)S(1)} collective-permute-done((f32[392,384]{1,0:T(8,128)S(1)}, f32[392,384]{1,0:T(8,128)S(1)}, u32[]{:S(2)}, u32[]{:S(2)}) %collective-permute-start.9) | collective-permute-done | bytes 602144 | tf_op jit(solution)/shard_map/ppermute | solution.py:186
  42.1 0.2 finish.1
  42.3 8.5 %all_to_all.19 = bf16[2,192,384]{2,1,0:T(8,128)(2,1)S(1)} all-to-all(bf16[2,192,384]{2,1,0:T(8,128)(2,1)S(1)} %bitcast.21), channel_id=1, replica_groups=mesh['seq'=16,'head'=2] {'head'}, dimensions={0} | all-to-all | bytes 589824 | tf_op jit(solution)/shard_map/all_to_all | solution.py:276
  50.8 0.7 %copy.6 = bf16[2,24,8,384]{3,2,0,1:T(8,128)(2,1)} copy(bf16[2,24,8,384]{3,2,1,0:T(8,128)(2,1)S(1)} %bitcast.22) | data formatting | bytes 589824 | tf_op jit(solution)/shard_map/all_to_all | solution.py:276
Async XLA Ops:
  0.0 1.0 %copy-start = (bf16[384,384]{1,0:T(8,128)(2,1)S(1)}, bf16[384,384]{1,0:T(8,128)(2,1)}, u32[]{:S(2)}) copy-start(bf16[384,384]{1,0:T(8,128)(2,1)} %k_ref.1) | copy-start | bytes 884740
  1.0 1.0 %copy-start.1 = (bf16[384,384]{1,0:T(8,128)(2,1)S(1)}, bf16[384,384]{1,0:T(8,128)(2,1)}, u32[]{:S(2)}) copy-start(bf16[384,384]{1,0:T(8,128)(2,1)} %v_ref.1) | copy-start | bytes 884740
  1.9 20.4 %copy-start.2 = (bf16[384,384]{1,0:T(8,128)(2,1)S(1)}, bf16[384,384]{1,0:T(8,128)(2,1)}, u32[]{:S(2)}) copy-start(bf16[384,384]{1,0:T(8,128)(2,1)} %refs_0_.3) | copy-start | bytes 884740
  2.1 15.1 %collective-permute-start.6 = (bf16[768,384]{1,0:T(8,128)(2,1)S(1)}, bf16[768,384]{1,0:T(8,128)(2,1)S(1)}, u32[]{:S(2)}, u32[]{:S(2)}) collective-permute-start(bf16[768,384]{1,0:T(8,128)(2,1)S(1)} %pack.1.refs_2_), channel_id=1, source_target_pairs={{4,0},{6,2},{0,4},{2,6},{12,8},{14,10},{8,12},{10,14},{20,16},{22,... | collective-permute-start | bytes 1769480 | tf_op jit(solution)/shard_map/ppermute | solution.py:186
  3.7 16.7 %collective-permute-start.4 = (bf16[768,384]{1,0:T(8,128)(2,1)S(1)}, bf16[768,384]{1,0:T(8,128)(2,1)S(1)}, u32[]{:S(2)}, u32[]{:S(2)}) collective-permute-start(bf16[768,384]{1,0:T(8,128)(2,1)S(1)} %pack.1.refs_2_), channel_id=1, source_target_pairs={{8,0},{10,2},{16,8},{18,10},{4,12},{6,14},{24,16},{26,18},{12,20},... | collective-permute-start | bytes 1769480 | tf_op jit(solution)/shard_map/ppermute | solution.py:186
  6.0 22.3 %collective-permute-start.8 = (bf16[768,384]{1,0:T(8,128)(2,1)S(1)}, bf16[768,384]{1,0:T(8,128)(2,1)S(1)}, u32[]{:S(2)}, u32[]{:S(2)}) collective-permute-start(bf16[768,384]{1,0:T(8,128)(2,1)S(1)} %pack.1.refs_2_), channel_id=1, source_target_pairs={{12,4},{14,6},{0,8},{2,10},{20,12},{22,14},{8,16},{10,18},{28,20},... | collective-permute-start | bytes 1769480 | tf_op jit(solution)/shard_map/ppermute | solution.py:186
  17.2 18.2 %collective-permute-start.7 = (bf16[768,384]{1,0:T(8,128)(2,1)S(1)}, bf16[768,384]{1,0:T(8,128)(2,1)S(1)}, u32[]{:S(2)}, u32[]{:S(2)}) collective-permute-start(bf16[768,384]{1,0:T(8,128)(2,1)S(1)} %collective-permute-done.6.refs_4_), channel_id=1, source_target_pairs={{8,0},{10,2},{16,8},{18,10},{4,12},{6,14},{24,16},{26,18},{12,20},... | collective-permute-start | bytes 1769480 | tf_op jit(solution)/shard_map/ppermute | solution.py:186
  20.3 15.0 %collective-permute-start.5 = (bf16[768,384]{1,0:T(8,128)(2,1)S(1)}, bf16[768,384]{1,0:T(8,128)(2,1)}, u32[]{:S(2)}, u32[]{:S(2)}) collective-permute-start(bf16[768,384]{1,0:T(8,128)(2,1)S(1)} %collective-permute-done.4.refs_2_), channel_id=1, source_target_pairs={{4,0},{6,2},{0,4},{2,6},{12,8},{14,10},{8,12},{10,14},{20,16},{22,... | collective-permute-start | bytes 1769480 | tf_op jit(solution)/shard_map/ppermute | solution.py:186
  22.3 2.2 %collective-permute-start.3 = (bf16[384,384]{1,0:T(8,128)(2,1)S(1)}, bf16[384,384]{1,0:T(8,128)(2,1)S(1)}, u32[]{:S(2)}, u32[]{:S(2)}) collective-permute-start(bf16[384,384]{1,0:T(8,128)(2,1)S(1)} %copy-done.2), channel_id=1, source_target_pairs={{2,0},{0,2},{6,4},{4,6},{10,8},{8,10},{14,12},{12,14},{18,16},{16,... | collective-permute-start | bytes 884744 | tf_op jit(solution)/shard_map/ppermute | solution.py:186
  22.3 0.7 %copy-start.3 = (s32[5]{0:T(128)S(1)}, s32[5]{0:T(128)}, u32[]{:S(2)}) copy-start(s32[5]{0:T(128)} %tiles_ref.3) | copy-start | bytes 64
  40.0 2.1 %collective-permute-start.9 = (f32[392,384]{1,0:T(8,128)S(1)}, f32[392,384]{1,0:T(8,128)S(1)}, u32[]{:S(2)}, u32[]{:S(2)}) collective-permute-start(f32[392,384]{1,0:T(8,128)S(1)} %get-tuple-element.95), channel_id=1, source_target_pairs={{2,0},{0,2},{6,4},{4,6},{10,8},{8,10},{14,12},{12,14},{18,16},{16,... | collective-permute-start | bytes 1806344 | tf_op jit(solution)/shard_map/ppermute | solution.py:186
where the time goes:
time: 51.6 us; the launch traced here: 51.5 us
  Pallas kernels  15.5 us (30%)
  starting transfers between devices  11.8 us (23%)
  waiting for transfers between devices  10.5 us (20%)
  blocking collectives  8.47 us (16%)
  local copies, waits for them, and re-layouts  3.41 us (7%)
  other arithmetic  0.83 us (2%)
  between operations  0.75 us (1%)
    pallas_call x3, Pallas kernels, attend(): pl.pallas_call(functools.partial(attend_kernel, halves, slots, fresh, row...  15.2 us
    ppermute x7, starting transfers between devices, moved(): lax.ppermute(array, 'seq', [(source(s), s) for s in every if 0 <= source(...  11.8 us
    ppermute x7, waiting for transfers between devices, moved(): lax.ppermute(array, 'seq', [(source(s), s) for s in every if 0 <= source(...  10.5 us
    all_to_all x1, blocking collectives, shards(): lax.all_to_all(attended, 'head', split_axis=0, concat_axis=1, tiled=True)  8.47 us
    unnamed x8, local copies, waits for them, and re-layouts  2.58 us
  transfers between devices with their start and end apart: 7, of which 3 were waited for; matrix products, arithmetic and copies ran while one was open for 2% of the time, Pallas kernels for 21%

commit v1 on v0

v1 whole, which is shorter than its diff:
```python
import functools
import math

import jax
import jax.numpy as jnp
from jax import lax
from jax.experimental import pallas as pl
from jax.experimental.pallas import tpu as pltpu
from jax.sharding import PartitionSpec as P

HEAD_DIM = 128
TILE = 128
MOST_TILES = 21

LOWEST = -1e30
SCALE2 = math.log2(math.e) / math.sqrt(HEAD_DIM)
COST = 6

VMEM = pl.BlockSpec(memory_space=pltpu.VMEM)
SMEM = pl.BlockSpec(memory_space=pltpu.SMEM)
HBM = pl.BlockSpec(memory_space=pl.ANY)


def params():
    return pltpu.CompilerParams(vmem_limit_bytes=32 * 1024 * 1024)


def head_columns(h):
    return slice(h * HEAD_DIM, (h + 1) * HEAD_DIM)


def image_bounds(tiles_ref, tile):
    first = jnp.int32(0)
    start, end = jnp.int32(0), jnp.int32(0)
    for i in range(tiles_ref.shape[0]):
        after = first + tiles_ref[i]
        inside = (tile >= first) & (tile < after)
        start = jnp.where(inside, first, start)
        end = jnp.where(inside, after, end)
        first = after
    return start, end


def chip_spans(tiles_ref, chip_tiles):
    first = jnp.int32(0)
    spans = jnp.int32(0)
    for i in range(tiles_ref.shape[0]):
        after = first + tiles_ref[i]
        low, high = first // chip_tiles, (after - 1) // chip_tiles
        odd = low + 1 - low % 2
        far = jnp.where(high - low >= 4, 2, jnp.where(high - odd >= 3, 1, 0))
        spans = jnp.maximum(spans, far)
        first = after
    return spans


def pack_kernel(halves, tiles_ref, places_ref, k_ref, v_ref, out_ref, bounds_ref, spans_ref, sems):
    rows = k_ref.shape[0]
    tiles = rows // TILE
    copies = [
        pltpu.make_async_copy(k_ref, out_ref.at[:rows], sems.at[0]),
        pltpu.make_async_copy(v_ref, out_ref.at[rows:], sems.at[1]),
    ]
    for copy in copies:
        copy.start()
    for half in range(halves):
        for at in range(tiles):
            start, end = image_bounds(tiles_ref, places_ref[half] * tiles + at)
            bounds_ref[2 * (half * tiles + at)] = start
            bounds_ref[2 * (half * tiles + at) + 1] = end
    spans_ref[0] = chip_spans(tiles_ref, 2 * tiles)
    for copy in copies:
        copy.wait()


def pack(halves, image_tiles, places, keys, values):
    rows, columns = keys.shape
    block, bounds, spans = pl.pallas_call(
        functools.partial(pack_kernel, halves),
        out_shape=[
            jax.ShapeDtypeStruct((2 * rows, columns), keys.dtype),
            jax.ShapeDtypeStruct((2 * halves * (rows // TILE),), jnp.int32),
            jax.ShapeDtypeStruct((1,), jnp.int32),
        ],
        in_specs=[SMEM, SMEM, HBM, HBM],
        out_specs=[VMEM, SMEM, SMEM],
        scratch_shapes=[pltpu.SemaphoreType.DMA((2,))],
        name="pack",
    )(image_tiles, places, keys, values)
    return block, bounds, spans[0]


def corner_kernel(places_ref, block_ref, out_ref):
    half = out_ref.shape[0] // 2
    skip = pl.multiple_of((places_ref[0] % 2) * TILE, TILE)
    out_ref[:half] = block_ref[pl.ds(skip, half)]
    out_ref[half:] = block_ref[pl.ds(block_ref.shape[0] // 2 + skip, half)]


def corner_of(places, block):
    return pl.pallas_call(
        corner_kernel,
        out_shape=jax.ShapeDtypeStruct((block.shape[0] - 2 * TILE, block.shape[1]), block.dtype),
        in_specs=[SMEM, VMEM],
        out_specs=VMEM,
        compiler_params=params(),
        name="corner",
    )(places, block)


def attend_kernel(halves, slots, fresh, bounds_ref, firsts_ref, *refs):
    q_refs, refs = refs[:halves], refs[halves:]
    slot_refs, refs = refs[: len(slots)], refs[len(slots) :]
    old_refs, refs = (None, refs) if fresh else (refs[:halves], refs[halves:])
    new_refs, (held_q, held, state) = refs[:halves], refs[halves:]
    rows, columns = q_refs[0].shape
    tiles = rows // TILE
    count = held.shape[1] // 2 // TILE
    heads = columns // HEAD_DIM

    for half in range(halves):
        held_q[half] = q_refs[half][...]
        if fresh:
            state[half, :, :columns] = jnp.zeros((rows, columns), jnp.float32)
            lane = lax.broadcasted_iota(jnp.int32, (rows, TILE), 1)
            state[half, :, columns:] = jnp.where(lane < heads, LOWEST, 0.0)
        else:
            state[half] = old_refs[half][...]
    for slot, ref in enumerate(slot_refs):
        held[slot] = ref[...]

    def fold(half, slot, first, starts, ends):
        for h in range(heads):
            own = head_columns(h)
            scores = lax.dot_general(
                held_q[half, :, own],
                held[slot, : count * TILE, own],
                (((1,), (1,)), ((), ())),
                preferred_element_type=jnp.float32,
            )
            max_at = slice(columns + h, columns + h + 1)
            total_at = slice(columns + heads + h, columns + heads + h + 1)
            rounded, factors = [], []
            for t in range(tiles):
                at = slice(t * TILE, (t + 1) * TILE)
                parts = []
                for j in range(count):
                    inside = (first + j >= starts[t]) & (first + j < ends[t])
                    off = jnp.where(inside, 0.0, 2 * LOWEST).astype(jnp.float32)
                    parts.append(scores[at, j * TILE : (j + 1) * TILE] * SCALE2 + off)
                old_max = state[half, at, max_at]
                new_max = jnp.maximum(old_max, jnp.max(functools.reduce(jnp.maximum, parts), axis=1, keepdims=True))
                weights = [jnp.exp2(part - new_max) for part in parts]
                factor = jnp.exp2(old_max - new_max)
                total = jnp.sum(functools.reduce(jnp.add, weights), axis=1, keepdims=True)
                state[half, at, max_at] = new_max
                state[half, at, total_at] = state[half, at, total_at] * factor + total
                factors.append(factor)
                rounded.append(jnp.concatenate([w.astype(jnp.bfloat16) for w in weights], axis=1))
            update = jnp.dot(
                jnp.concatenate(rounded, axis=0),
                held[slot, count * TILE :, own],
                preferred_element_type=jnp.float32,
            )
            for t in range(tiles):
                at = slice(t * TILE, (t + 1) * TILE)
                state[half, at, own] = state[half, at, own] * factors[t] + update[at]

    firsts = [firsts_ref[at] for at in slots]

    @pl.loop(0, halves * len(slots))
    def _(unit):
        half, slot = unit // len(slots), unit % len(slots)
        first = firsts[0]
        for i in range(1, len(slots)):
            first = jnp.where(slot == i, firsts[i], first)
        starts = [bounds_ref[2 * (half * tiles + t)] for t in range(tiles)]
        ends = [bounds_ref[2 * (half * tiles + t) + 1] for t in range(tiles)]

        @pl.when((first < ends[-1]) & (first + count > starts[0]))
        def _():
            fold(half, slot, first, starts, ends)

    for half in range(halves):
        new_refs[half][...] = state[half]


def attend(bounds, firsts, queries, blocks, slots, states):
    halves = len(queries)
    rows, columns = queries[0].shape
    heads = columns // HEAD_DIM
    shape = jax.ShapeDtypeStruct((rows, columns + TILE), jnp.float32)
    pairs = halves * (rows // TILE) * heads * sum(b.shape[0] // 2 // TILE for b in blocks)
    return pl.pallas_call(
        functools.partial(attend_kernel, halves, slots, not states),
        out_shape=[shape] * halves,
        in_specs=[SMEM, SMEM] + [VMEM] * (halves + len(blocks) + len(states)),
        out_specs=[VMEM] * halves,
        scratch_shapes=[
            pltpu.VMEM((halves, rows, columns), queries[0].dtype),
            pltpu.VMEM((len(blocks),) + blocks[0].shape, blocks[0].dtype),
            pltpu.VMEM((halves, rows, columns + TILE), jnp.float32),
        ],
        compiler_params=params(),
        cost_estimate=pl.CostEstimate(
            flops=COST * pairs * 4 * TILE * TILE * HEAD_DIM,
            bytes_accessed=len(blocks) * rows * columns * 4 + 4 * halves * rows * (columns + TILE),
            transcendentals=pairs * TILE * TILE,
        ),
        name="attend",
    )(bounds, firsts, *queries, *blocks, *states)


def merged(states, rows, columns):
    heads = columns // HEAD_DIM
    for h in range(heads):
        maxima = [ref[rows, columns + h : columns + h + 1] for ref in states]
        totals = [ref[rows, columns + heads + h : columns + heads + h + 1] for ref in states]
        largest = functools.reduce(jnp.maximum, maxima)
        factors = [jnp.exp2(m - largest) for m in maxima]
        total = functools.reduce(jnp.add, [f * t for f, t in zip(factors, totals)])
        parts = [ref[rows, head_columns(h)] * (f / total) for ref, f in zip(states, factors)]
        yield head_columns(h), functools.reduce(jnp.add, parts)


def finish_kernel(*refs):
    out_ref = refs[-1]
    for own, done in merged(refs[:-1], slice(None), out_ref.shape[1]):
        out_ref[:, own] = done.astype(out_ref.dtype)


def finish(states, columns):
    return pl.pallas_call(
        finish_kernel,
        out_shape=jax.ShapeDtypeStruct((states[0].shape[0], columns), jnp.bfloat16),
        in_specs=[VMEM] * len(states),
        out_specs=VMEM,
        compiler_params=params(),
        name="finish",
    )(*states)


def part_kernel(places_ref, *refs):
    keep_ref, send_ref = refs[-2:]
    rows, columns = keep_ref.shape
    mine = places_ref[2]
    for out_ref, which in ((send_ref, 1 - mine), (keep_ref, mine)):
        there = pl.ds(pl.multiple_of(which * rows, 16), rows)
        for own, done in merged(refs[:-2], there, columns):
            out_ref[:, own] = done.astype(out_ref.dtype)


def join_kernel(places_ref, keep_ref, got_ref, out_ref):
    columns = keep_ref.shape[1]
    mine = places_ref[2]
    out_ref[:, pl.ds(pl.multiple_of(mine * columns, TILE), columns)] = keep_ref[...]
    out_ref[:, pl.ds(pl.multiple_of((1 - mine) * columns, TILE), columns)] = got_ref[...]


def finish_in_two(places, states, columns):
    rows = states[0].shape[0]
    part = jax.ShapeDtypeStruct((rows // 2, columns), jnp.bfloat16)
    keep, send = pl.pallas_call(
        part_kernel,
        out_shape=[part, part],
        in_specs=[SMEM] + [VMEM] * len(states),
        out_specs=[VMEM, VMEM],
        compiler_params=params(),
        name="part",
    )(places, *states)
    got = lax.ppermute(send, "head", [(0, 1), (1, 0)])
    return pl.pallas_call(
        join_kernel,
        out_shape=jax.ShapeDtypeStruct((rows // 2, 2 * columns), jnp.bfloat16),
        in_specs=[SMEM, VMEM, VMEM],
        out_specs=VMEM,
        compiler_params=params(),
        name="join",
    )(places, keep, got)


def chip_pairs(mesh):
    places = [tuple(getattr(d, "coords", ())) for d in mesh.devices[:, 0]]
    count = len(places)
    if count % 4 or not places[0] or mesh.shape["head"] != 2:
        return False
    cores = all(places[i] == places[i + 1] for i in range(0, count, 2))
    level = all(places[i][2] == places[i + 3][2] for i in range(0, count, 4))
    climb = all(places[i][2] != places[i + 4][2] for i in range(0, count - 4))
    return cores and level and climb


def paired_shards(owner_count, queries, keys, values, image_tiles):
    rows, columns = queries.shape
    tiles = rows // TILE
    every = range(owner_count)

    def sign(s):
        return 1 - 2 * ((s // 2) % 2)

    def moved(array, source):
        return lax.ppermute(array, "seq", [(source(s), s) for s in every if 0 <= source(s) < owner_count])

    along = lambda s: s + 4 * sign(s)
    against = lambda s: s - 4 * sign(s)
    across = lambda s: s + 2 * sign(s)
    corner = lambda s: s + 8 * (1 - 2 * (s % 2))
    sibling = lambda s: s + 1 - 2 * (s % 2)

    me = lax.axis_index("seq")
    places = jnp.stack([me, sibling(me), lax.axis_index("head")]).astype(jnp.int32)
    owners = [me, along(me), against(me), across(me), me - 2 * sign(me), me + 6 * sign(me), me - 6 * sign(me)]
    firsts = jnp.stack([o * tiles for o in owners] + [corner(me) * tiles + me % 2]).astype(jnp.int32)
    OWN, A1, B1, Y1, YA, AY, BYA, CORNER = range(8)

    block, bounds, spans = pack(2, image_tiles, places, keys, values)
    y1, a1, b1 = moved(block, across), moved(block, along), moved(block, against)
    both = (queries, moved(queries, sibling))
    fold = functools.partial(attend, bounds, firsts, both)
    states = fold([block], [OWN], [])
    ya, ay = moved(a1, across), moved(y1, along)
    states = fold([a1, b1, y1], [A1, B1, Y1], states)

    def near(block, ya, ay, states):
        return fold([ya, ay], [YA, AY], states)

    def further(block, ya, ay, states):
        bya = moved(ya, against)
        states = fold([ya, ay], [YA, AY], states)
        return fold([bya], [BYA], states)

    def furthest(block, ya, ay, states):
        bya = moved(ya, against)
        far = moved(corner_of(places, block), corner)
        states = fold([ya, ay], [YA, AY], states)
        states = fold([bya], [BYA], states)
        return fold([far], [CORNER], states)

    mine, theirs = lax.switch(spans, [near, further, furthest], block, ya, ay, states)
    return finish_in_two(places, [mine, moved(theirs, sibling)], columns)


def ring_shards(owner_count, queries, keys, values, image_tiles):
    rows, columns = queries.shape
    tiles = rows // TILE
    reach = min(owner_count - 1, -(-(MOST_TILES - 1) // tiles))
    me = lax.axis_index("seq")
    places = jnp.stack([me, me, lax.axis_index("head")]).astype(jnp.int32)
    block, bounds, _ = pack(1, image_tiles, places, keys, values)
    firsts = jnp.stack([me + k for k in range(-reach, reach + 1)]).astype(jnp.int32) * tiles
    fold = functools.partial(attend, bounds, firsts, (queries,))
    up = [(i, i + 1) for i in range(owner_count - 1)]
    down = [(i + 1, i) for i in range(owner_count - 1)]
    below = above = block
    states = []
    held, slots = [block], [reach]
    for k in range(1, reach + 1):
        below = lax.ppermute(below, "seq", up)
        above = lax.ppermute(above, "seq", down)
        states = fold(held, slots, states)
        held, slots = [below, above], [reach - k, reach + k]
    attended = finish(fold(held, slots, states), columns)
    return lax.all_to_all(attended, "head", split_axis=0, concat_axis=1, tiled=True)


def solution(mesh):
    owner_count = mesh.shape["seq"]
    plan = paired_shards if chip_pairs(mesh) else ring_shards
    placed = (P("seq", "head"), P("seq", "head"), P("seq", "head"), P())
    return jax.shard_map(
        functools.partial(plan, owner_count),
        mesh=mesh,
        in_specs=placed,
        out_specs=P(("seq", "head"), None),
        check_vma=False,
    )
```

time: 51.6 us -> 54.9 us (1.064)
  the two profiles are of different devices: /device:TPU:16 before, /device:TPU:22 now
where the time goes in v1:
time: 54.9 us; the launch traced here: 54.6 us
  Pallas kernels  24.5 us (45%)
  waiting for transfers between devices  19.5 us (36%)
  starting transfers between devices  9.26 us (17%)
  between operations  0.8 us (1%)
    pallas_call x3, Pallas kernels, attend(): pl.pallas_call(functools.partial(attend_kernel, halves, slots, not states...  19.2 us
    ppermute x7, waiting for transfers between devices, moved(): lax.ppermute(array, 'seq', [(source(s), s) for s in every if 0 <= source(...  14.2 us
    ppermute x7, starting transfers between devices, moved(): lax.ppermute(array, 'seq', [(source(s), s) for s in every if 0 <= source(...  8.66 us
    ppermute x1, waiting for transfers between devices, finish_in_two(): got = lax.ppermute(send, 'head', [(0, 1), (1, 0)])  5.35 us
    pallas_call x1, Pallas kernels, pack(): pl.pallas_call(functools.partial(pack_kernel, halves), out_shape=[jax.Sha...  2.46 us
    pallas_call x1, Pallas kernels, finish_in_two(): pl.pallas_call(part_kernel, out_shape=[part, part], in_specs=[SMEM] + [VM...  1.64 us
    pallas_call x1, Pallas kernels, finish_in_two(): pl.pallas_call(join_kernel, out_shape=jax.ShapeDtypeStruct((rows // 2, 2...  1.28 us
  transfers between devices with their start and end apart: 8, of which 7 were waited for; matrix products, arithmetic and copies ran while one was open for 0% of the time, Pallas kernels for 23%

profile of v1, /device:TPU:22, one launch (start us, length us, event | category | flops | bytes accessed | tf_op | source)
XLA Modules:
  0.0 54.6 jit_solution(5781934304511890528)
XLA Ops:
  0.0 0.1 pad_add_fusion.places_ref
  0.1 0.0 copy-start
  0.1 2.5 %pack.1 = (bf16[768,384]{1,0:T(8,128)(2,1)S(1)}, s32[12]{0:T(128)S(1)}, s32[1]{0:T(128)}) custom-call(s32[5]{0:T(128)} %tiles_ref.1, s32[3]{0:T(128)S(1)} %pad_add_fusion.places_ref, bf16[384,384]{1,0:T(8,128)(2,1)} %k_ref.1, bf16[384,384]{1,0:T(8,128)(2,1)} %v_ref.1), custom_call_target="tpu_custom_call" | custom-call | tf_op jit(solution)/shard_map/pack/pallas_call | solution.py:78
  2.5 3.5 %collective-permute-start.4 = (bf16[768,384]{1,0:T(8,128)(2,1)S(1)}, bf16[768,384]{1,0:T(8,128)(2,1)S(1)}, u32[]{:S(2)}, u32[]{:S(2)}) collective-permute-start(bf16[768,384]{1,0:T(8,128)(2,1)S(1)} %get-tuple-element.102.refs_2_), channel_id=1, source_target_pairs={{8,0},{10,2},{16,8},{18,10},{4,12},{6,14},{24,16},{26,18},{12,20},... | collective-permute-start | bytes 1769480 | tf_op jit(solution)/shard_map/ppermute | solution.py:302
  6.0 0.1 collective-permute-start.6
  6.1 2.4 %collective-permute-start.8 = (bf16[768,384]{1,0:T(8,128)(2,1)S(1)}, bf16[768,384]{1,0:T(8,128)(2,1)S(1)}, u32[]{:S(2)}, u32[]{:S(2)}) collective-permute-start(bf16[768,384]{1,0:T(8,128)(2,1)S(1)} %get-tuple-element.102.refs_2_), channel_id=1, source_target_pairs={{12,4},{14,6},{0,8},{2,10},{20,12},{22,14},{8,16},{10,18},{28,20},... | collective-permute-start | bytes 1769480 | tf_op jit(solution)/shard_map/ppermute | solution.py:302
  8.5 0.0 copy-done
  8.5 0.1 collective-permute-start.3
  9.3 0.1 stack.51.firsts_ref
  9.4 0.8 %collective-permute-done.3.refs_1_ = bf16[384,384]{1,0:T(8,128)(2,1)S(1)} collective-permute-done((bf16[384,384]{1,0:T(8,128)(2,1)S(1)}, bf16[384,384]{1,0:T(8,128)(2,1)S(1)}, u32[]{:S(2)}, u32[]{:S(2)}) %collective-permute-start.3) | collective-permute-done | bytes 294944 | tf_op jit(solution)/shard_map/ppermute | solution.py:302
  10.1 6.3 %attend.14 = (f32[384,512]{1,0:T(8,128)S(1)}, f32[384,512]{1,0:T(8,128)S(1)}) custom-call(s32[12]{0:T(128)S(1)} %get-tuple-element.101.bounds_ref, s32[8]{0:T(128)S(1)} %stack.51.firsts_ref, bf16[384,384]{1,0:T(8,128)(2,1)S(1)} %copy-done, bf16[384,384]{1,0:T(8,128)(2,1)S(1)} %collective-permute-done.3.refs_1_, bf16[768,384]{1,0:T(8,128)(2,1)S(1)} %get-tuple-element.102.refs_2_), custom_call_target="tpu_custom_call" | custom-call | flops 2717908992 | bytes 2162688 | tf_op jit(solution)/shard_map/attend/pallas_call | solution.py:194
  16.4 3.1 %collective-permute-done.4.refs_2_ = bf16[768,384]{1,0:T(8,128)(2,1)S(1)} collective-permute-done((bf16[768,384]{1,0:T(8,128)(2,1)S(1)}, bf16[768,384]{1,0:T(8,128)(2,1)S(1)}, u32[]{:S(2)}, u32[]{:S(2)}) %collective-permute-start.4) | collective-permute-done | bytes 589856 | tf_op jit(solution)/shard_map/ppermute | solution.py:302
  19.5 0.5 collective-permute-start.5
  20.0 0.9 %collective-permute-done.6.refs_4_ = bf16[768,384]{1,0:T(8,128)(2,1)S(1)} collective-permute-done((bf16[768,384]{1,0:T(8,128)(2,1)S(1)}, bf16[768,384]{1,0:T(8,128)(2,1)S(1)}, u32[]{:S(2)}, u32[]{:S(2)}) %collective-permute-start.6) | collective-permute-done | bytes 589856 | tf_op jit(solution)/shard_map/ppermute | solution.py:302
  20.9 2.1 %collective-permute-start.7 = (bf16[768,384]{1,0:T(8,128)(2,1)S(1)}, bf16[768,384]{1,0:T(8,128)(2,1)S(1)}, u32[]{:S(2)}, u32[]{:S(2)}) collective-permute-start(bf16[768,384]{1,0:T(8,128)(2,1)S(1)} %collective-permute-done.6.refs_4_), channel_id=1, source_target_pairs={{8,0},{10,2},{16,8},{18,10},{4,12},{6,14},{24,16},{26,18},{12,20},... | collective-permute-start | bytes 1769480 | tf_op jit(solution)/shard_map/ppermute | solution.py:302
  23.0 0.0 collective-permute-done.8.refs_3_
  23.0 6.5 %attend.15 = (f32[384,512]{1,0:T(8,128)S(1)}, f32[384,512]{1,0:T(8,128)S(1)}) custom-call(s32[12]{0:T(128)S(1)} %get-tuple-element.101.bounds_ref, s32[8]{0:T(128)S(1)} %stack.51.firsts_ref, bf16[384,384]{1,0:T(8,128)(2,1)S(1)} %copy-done, bf16[384,384]{1,0:T(8,128)(2,1)S(1)} %collective-permute-done.3.refs_1_, ...), custom_call_target="tpu_custom_call" | custom-call | flops 8153726976 | bytes 3342336 | tf_op jit(solution)/shard_map/attend/pallas_call | solution.py:194
  29.5 4.2 %collective-permute-done.5 = bf16[768,384]{1,0:T(8,128)(2,1)S(1)} collective-permute-done((bf16[768,384]{1,0:T(8,128)(2,1)S(1)}, bf16[768,384]{1,0:T(8,128)(2,1)S(1)}, u32[]{:S(2)}, u32[]{:S(2)}) %collective-permute-start.5) | collective-permute-done | bytes 589856 | tf_op jit(solution)/shard_map/ppermute | solution.py:302
  33.7 2.9 %collective-permute-done.7 = bf16[768,384]{1,0:T(8,128)(2,1)S(1)} collective-permute-done((bf16[768,384]{1,0:T(8,128)(2,1)S(1)}, bf16[768,384]{1,0:T(8,128)(2,1)S(1)}, u32[]{:S(2)}, u32[]{:S(2)}) %collective-permute-start.7) | collective-permute-done | bytes 589856 | tf_op jit(solution)/shard_map/ppermute | solution.py:302
  36.7 6.7 %conditional.1 = ((f32[384,512]{1,0:T(8,128)S(1)}, f32[384,512]{1,0:T(8,128)S(1)})) conditional(s32[]{:T(128)} %bitcast.3, (s32[12]{0:T(128)S(1)}, s32[8]{0:T(128)S(1)}, bf16[384,384]{1,0:T(8,128)(2,1)S(1)}, bf16[384,384]{1,0:T(8,128)(2,1)S(1)}, bf16[768,384]{1,0:T(8,128)(2,1)S(1)}, /*index=5*/bf16[768,384]{1,0:T(8,128)(2,1)S(1)}, ...), branch_computations={%region_0.1_spmd, %region_1.2_spmd, %region_2.3_spmd} | conditional | flops 9965666304 | bytes 17301648 | solution.py:339
  36.7 6.4 %attend.8 = (f32[384,512]{1,0:T(8,128)S(1)}, f32[384,512]{1,0:T(8,128)S(1)}) custom-call(s32[12]{0:T(128)S(1)} %get-tuple-element.57.bounds_ref, s32[8]{0:T(128)S(1)} %get-tuple-element.58.firsts_ref, bf16[384,384]{1,0:T(8,128)(2,1)S(1)} %get-tuple-element.59.refs_0_, bf16[384,384]{1,0:T(8,128)(2,1)S(1)} %get-tuple-element.60.refs_1_, ...), custom_call_target="tpu_custom_call" | custom-call | flops 5435817984 | bytes 2752512 | tf_op jit(solution)/shard_map/cond/branch_0_fun/attend/pallas_call | solution.py:194
  43.3 0.1 collective-permute-start.9
  43.4 2.3 %collective-permute-done.9.refs_1_ = f32[384,512]{1,0:T(8,128)S(1)} collective-permute-done((f32[384,512]{1,0:T(8,128)S(1)}, f32[384,512]{1,0:T(8,128)S(1)}, u32[]{:S(2)}, u32[]{:S(2)}) %collective-permute-start.9) | collective-permute-done | bytes 786464 | tf_op jit(solution)/shard_map/ppermute | solution.py:302
  45.7 1.6 %part.1 = (bf16[192,384]{1,0:T(8,128)(2,1)S(1)}, bf16[192,384]{1,0:T(8,128)(2,1)S(1)}) custom-call(s32[3]{0:T(128)S(1)} %pad_add_fusion.places_ref, f32[384,512]{1,0:T(8,128)S(1)} %get-tuple-element.107.refs_0_, f32[384,512]{1,0:T(8,128)S(1)} %collective-permute-done.9.refs_1_), custom_call_target="tpu_custom_call" | custom-call | tf_op jit(solution)/shard_map/part/pallas_call | solution.py:263
  47.3 0.6 %collective-permute-start.10 = (bf16[192,384]{1,0:T(8,128)(2,1)S(1)}, bf16[192,384]{1,0:T(8,128)(2,1)S(1)}, u32[]{:S(2)}, u32[]{:S(2)}) collective-permute-start(bf16[192,384]{1,0:T(8,128)(2,1)S(1)} %get-tuple-element.110), channel_id=1, source_target_pairs={{0,1},{1,0},{2,3},{3,2},{4,5},{5,4},{6,7},{7,6},{8,9},{9,8},{10,11... | collective-permute-start | bytes 442376 | tf_op jit(solution)/shard_map/ppermute | solution.py:271
  47.9 5.4 %collective-permute-done.10.got_ref = bf16[192,384]{1,0:T(8,128)(2,1)S(1)} collective-permute-done((bf16[192,384]{1,0:T(8,128)(2,1)S(1)}, bf16[192,384]{1,0:T(8,128)(2,1)S(1)}, u32[]{:S(2)}, u32[]{:S(2)}) %collective-permute-start.10) | collective-permute-done | bytes 147488 | tf_op jit(solution)/shard_map/ppermute | solution.py:271
  53.3 1.3 %join.1 = bf16[192,768]{1,0:T(8,128)(2,1)} custom-call(s32[3]{0:T(128)S(1)} %pad_add_fusion.places_ref, bf16[192,384]{1,0:T(8,128)(2,1)S(1)} %get-tuple-element.109.keep_ref, bf16[192,384]{1,0:T(8,128)(2,1)S(1)} %collective-permute-done.10.got_ref), custom_call_target="tpu_custom_call" | custom-call | tf_op jit(solution)/shard_map/join/pallas_call | solution.py:272
Async XLA Ops:
  0.1 8.4 %copy-start = (bf16[384,384]{1,0:T(8,128)(2,1)S(1)}, bf16[384,384]{1,0:T(8,128)(2,1)}, u32[]{:S(2)}) copy-start(bf16[384,384]{1,0:T(8,128)(2,1)} %refs_0_.3) | copy-start | bytes 884740
  2.5 17.0 %collective-permute-start.4 = (bf16[768,384]{1,0:T(8,128)(2,1)S(1)}, bf16[768,384]{1,0:T(8,128)(2,1)S(1)}, u32[]{:S(2)}, u32[]{:S(2)}) collective-permute-start(bf16[768,384]{1,0:T(8,128)(2,1)S(1)} %get-tuple-element.102.refs_2_), channel_id=1, source_target_pairs={{8,0},{10,2},{16,8},{18,10},{4,12},{6,14},{24,16},{26,18},{12,20},... | collective-permute-start | bytes 1769480 | tf_op jit(solution)/shard_map/ppermute | solution.py:302
  6.0 14.9 %collective-permute-start.6 = (bf16[768,384]{1,0:T(8,128)(2,1)S(1)}, bf16[768,384]{1,0:T(8,128)(2,1)S(1)}, u32[]{:S(2)}, u32[]{:S(2)}) collective-permute-start(bf16[768,384]{1,0:T(8,128)(2,1)S(1)} %get-tuple-element.102.refs_2_), channel_id=1, source_target_pairs={{4,0},{6,2},{0,4},{2,6},{12,8},{14,10},{8,12},{10,14},{20,16},{22,... | collective-permute-start | bytes 1769480 | tf_op jit(solution)/shard_map/ppermute | solution.py:302
  6.1 16.9 %collective-permute-start.8 = (bf16[768,384]{1,0:T(8,128)(2,1)S(1)}, bf16[768,384]{1,0:T(8,128)(2,1)S(1)}, u32[]{:S(2)}, u32[]{:S(2)}) collective-permute-start(bf16[768,384]{1,0:T(8,128)(2,1)S(1)} %get-tuple-element.102.refs_2_), channel_id=1, source_target_pairs={{12,4},{14,6},{0,8},{2,10},{20,12},{22,14},{8,16},{10,18},{28,20},... | collective-permute-start | bytes 1769480 | tf_op jit(solution)/shard_map/ppermute | solution.py:302
  8.5 1.6 %collective-permute-start.3 = (bf16[384,384]{1,0:T(8,128)(2,1)S(1)}, bf16[384,384]{1,0:T(8,128)(2,1)S(1)}, u32[]{:S(2)}, u32[]{:S(2)}) collective-permute-start(bf16[384,384]{1,0:T(8,128)(2,1)S(1)} %copy-done), channel_id=1, source_target_pairs={{2,0},{0,2},{6,4},{4,6},{10,8},{8,10},{14,12},{12,14},{18,16},{16,... | collective-permute-start | bytes 884744 | tf_op jit(solution)/shard_map/ppermute | solution.py:302
  19.5 14.2 %collective-permute-start.5 = (bf16[768,384]{1,0:T(8,128)(2,1)S(1)}, bf16[768,384]{1,0:T(8,128)(2,1)S(1)}, u32[]{:S(2)}, u32[]{:S(2)}) collective-permute-start(bf16[768,384]{1,0:T(8,128)(2,1)S(1)} %collective-permute-done.4.refs_2_), channel_id=1, source_target_pairs={{4,0},{6,2},{0,4},{2,6},{12,8},{14,10},{8,12},{10,14},{20,16},{22,... | collective-permute-start | bytes 1769480 | tf_op jit(solution)/shard_map/ppermute | solution.py:302
  20.9 15.8 %collective-permute-start.7 = (bf16[768,384]{1,0:T(8,128)(2,1)S(1)}, bf16[768,384]{1,0:T(8,128)(2,1)S(1)}, u32[]{:S(2)}, u32[]{:S(2)}) collective-permute-start(bf16[768,384]{1,0:T(8,128)(2,1)S(1)} %collective-permute-done.6.refs_4_), channel_id=1, source_target_pairs={{8,0},{10,2},{16,8},{18,10},{4,12},{6,14},{24,16},{26,18},{12,20},... | collective-permute-start | bytes 1769480 | tf_op jit(solution)/shard_map/ppermute | solution.py:302
  43.3 2.4 %collective-permute-start.9 = (f32[384,512]{1,0:T(8,128)S(1)}, f32[384,512]{1,0:T(8,128)S(1)}, u32[]{:S(2)}, u32[]{:S(2)}) collective-permute-start(f32[384,512]{1,0:T(8,128)S(1)} %get-tuple-element.108), channel_id=1, source_target_pairs={{2,0},{0,2},{6,4},{4,6},{10,8},{8,10},{14,12},{12,14},{18,16},{16,... | collective-permute-start | bytes 2359304 | tf_op jit(solution)/shard_map/ppermute | solution.py:302
  47.3 6.0 %collective-permute-start.10 = (bf16[192,384]{1,0:T(8,128)(2,1)S(1)}, bf16[192,384]{1,0:T(8,128)(2,1)S(1)}, u32[]{:S(2)}, u32[]{:S(2)}) collective-permute-start(bf16[192,384]{1,0:T(8,128)(2,1)S(1)} %get-tuple-element.110), channel_id=1, source_target_pairs={{0,1},{1,0},{2,3},{3,2},{4,5},{5,4},{6,7},{7,6},{8,9},{9,8},{10,11... | collective-permute-start | bytes 442376 | tf_op jit(solution)/shard_map/ppermute | solution.py:271
